TPU v7x, 32 devices: a whole 2x2x4 slice. The times are simulated.
32 devices in a mesh: groups: 2 (over y), ao: 4 (over z), aux: 2 (over x), occ: 2 (over core).
Axes of the slice: x: 2, y: 2, z: 4, core: 2. Of those that a mesh axis runs over, the one named last changes fastest.
Arguments:
- slab: bfloat16 [40, 3072, 3072], P(('groups', 'aux'), 'ao'), parts along dimension 0, may hold values from -6 to 6
- coeffs: bfloat16 [6144, 384], P(('groups', 'ao')), parts along dimension 0, may hold values from -0.109375 to 0.109375
- atom_of: int32 [6144], P(('groups', 'ao')), parts along dimension 0, may hold values from 0 to 399, never falling along the last dimension, each value on 1 to 16 neighbouring positions
Outputs:
- gradient: float32 [6144, 384], P(('groups', 'ao'), ('aux', 'occ')), parts along dimension 0
- atom_energy: float32 [800], P('groups'), parts along dimension 0
There are 2 independent parts, one for each index of `groups`. A program takes and returns all parts, laid end to end along the dimension named above; each array names one. Nothing has to cross between parts.
Inputs may be any that keep to these rules, and one draw needn't show every extreme that they name: atom_of never falls along the basis functions; each atom holds 1 to 16 functions, and some atom exactly 16.
All inputs are finite; a program needn't handle non-finite values.
Results may differ from a plain program's by a relative error of at most 0.0027.
Values may be sent and summed in bfloat16 or wider, within the bound.
A program may use at most 128 MiB of HBM per device.

v0:
```python
import jax
import jax.numpy as jnp
from jax import lax
from jax.sharding import PartitionSpec as P

NATOM = 400


def shards(slab, coeffs, atom_of):
    coeff_all = lax.all_gather(coeffs, "ao", axis=0, tiled=True)
    total_occ = coeff_all.shape[1]
    half_width = total_occ // lax.axis_size("occ")
    offset = lax.axis_index("occ") * half_width
    own_cols = lax.dynamic_slice_in_dim(coeff_all, offset, half_width, 1)
    half = jnp.einsum("pmn,ni->pim", slab, own_cols, preferred_element_type=jnp.float32).astype(
        jnp.bfloat16
    )
    pair_block = jnp.einsum(
        "pim,mj->pij",
        lax.all_to_all(half, "ao", split_axis=1, concat_axis=2, tiled=True),
        coeff_all,
        preferred_element_type=jnp.float32,
    )
    pair_block = pair_block.astype(jnp.bfloat16)
    accum_total = jnp.einsum(
        "pim,pij->mj",
        half,
        lax.all_gather(pair_block, "ao", axis=1, tiled=True),
        preferred_element_type=jnp.float32,
    )
    aux_total = slab.shape[0] * lax.axis_size("aux")
    normalizer = 1.0 / jnp.sqrt(jnp.float32(aux_total * total_occ))
    gradient = lax.psum_scatter(
        accum_total * normalizer, ("aux", "occ"), scatter_dimension=1, tiled=True
    )
    col_width = gradient.shape[1]
    col_offset = lax.axis_index(("aux", "occ")) * col_width
    own_coeffs = lax.dynamic_slice_in_dim(coeffs, col_offset, col_width, 1).astype(jnp.float32)
    weighted = jnp.sum(own_coeffs * gradient, axis=1)
    onehot = (atom_of[:, None] == jnp.arange(NATOM, dtype=jnp.int32)[None, :]).astype(jnp.float32)
    atom_part = jnp.dot(weighted, onehot, precision=lax.Precision.HIGHEST)
    atom_energy = lax.psum(atom_part, ("ao", "aux", "occ"))
    return (gradient, atom_energy)


def solution(mesh):
    in_specs = (P(("groups", "aux"), "ao", None), P(("groups", "ao"), None), P(("groups", "ao")))
    out_specs = (P(("groups", "ao"), ("aux", "occ")), P("groups"))
    return jax.shard_map(shards, mesh=mesh, in_specs=in_specs, out_specs=out_specs, check_vma=False)
```

profile of v0, /device:TPU:0, one launch (start us, length us, event | category | flops | bytes accessed | tf_op | source)
XLA Modules:
  0.0 308.5 jit_solution(14513100436666991084)
XLA Ops:
  7.2 0.0 all-gather.3.cloned.1.call-start
  7.2 2.2 copy.10
  9.4 0.0 all-gather.3.cloned.1.call-update
  9.4 0.0 all-gather.5.cloned.1.call-start
  9.5 53.3 %all-gather.3.cloned.1.call-done = bf16[3072,384]{0,1:T(8,128)(2,1)} async-done(((bf16[768,384]{0,1:T(8,128)(2,1)}), bf16[3072,384]{0,1:T(8,128)(2,1)}) %all-gather.3.cloned.1.call-update) | async-done | bytes 2359312 | tf_op jit(solution)/shard_map/all_gather | solution.py:10
  62.7 21.2 %convert_bitcast_fusion = bf16[10,192,768]{2,1,0:T(8,128)(2,1)S(1)} fusion(bf16[10,768,3072]{2,1,0:T(8,128)(2,1)} %param.3, bf16[3072,384]{0,1:T(8,128)(2,1)} %all-gather.3.cloned.1.call-done, s32[]{:T(128)S(6)} %select_n.6), kind=kOutput, calls=%fused_computation.1 | convolution fusion | flops 9061171200 | bytes 51314692 | tf_op jit(solution)/shard_map/pmn,ni->pim/dot_general | solution.py:15
  83.9 0.0 copy-start
  83.9 1.8 copy.11
  85.7 0.0 copy-done
  85.7 107.2 %all_to_all.18 = bf16[10,192,768]{2,0,1:T(8,128)(2,1)S(1)} all-to-all(bf16[10,192,768]{2,0,1:T(8,128)(2,1)S(1)} %copy.11), channel_id=1, replica_groups=mesh['groups'=2,'ao'=4,'aux'=2,'occ'=2] {'ao'}, dimensions={1} | all-to-all | bytes 5898240 | tf_op jit(solution)/shard_map/all_to_all | solution.py:20
  192.9 2.3 copy.18
  195.2 3.8 %all_to_all.16 = bf16[10,48,3072]{2,1,0:T(8,128)(2,1)} reshape(bf16[10,48,4,768]{3,2,1,0:T(4,128)(2,1)S(1)} %bitcast.25) | data formatting | bytes 5898240 | tf_op jit(solution)/shard_map/all_to_all | solution.py:20
  199.0 0.0 copy-start.1
  199.0 5.2 %fusion.4 = bf16[10,48,384]{2,1,0:T(8,128)(2,1)} fusion(bf16[10,48,3072]{2,1,0:T(8,128)(2,1)} %all_to_all.16, bf16[3072,384]{0,1:T(8,128)(2,1)} %all-gather.3.cloned.1.call-done), kind=kOutput, calls=%fused_computation.8 | convolution fusion | flops 1132646400 | bytes 5677056 | tf_op jit(solution)/shard_map/pim,mj->pij/dot_general | solution.py:18
  204.2 0.0 all-gather.5.cloned.1.call-update
  204.2 0.0 copy-start.2
  204.3 0.0 reduce-scatter.2.cloned.1.call-start
  204.3 34.6 %all-gather.5.cloned.1.call-done = bf16[10,192,384]{2,1,0:T(8,128)(2,1)} async-done(((bf16[10,48,384]{2,1,0:T(8,128)(2,1)}), bf16[10,192,384]{2,1,0:T(8,128)(2,1)}) %all-gather.5.cloned.1.call-update) | async-done | bytes 1474576 | tf_op jit(solution)/shard_map/all_gather | solution.py:28
  238.9 0.0 copy-done.1
  238.9 3.8 %fusion.3 = f32[768,384]{0,1:T(8,128)} fusion(bf16[10,192,768]{2,1,0:T(8,128)(2,1)S(1)} %copy-done.1, bf16[10,192,384]{2,1,0:T(8,128)(2,1)} %all-gather.5.cloned.1.call-done), kind=kOutput, calls=%fused_computation.7 | convolution fusion | flops 1132756992 | bytes 5603328 | tf_op jit(solution)/shard_map/pim,pij->mj/dot_general | solution.py:25
  242.7 0.0 reduce-scatter.2.cloned.1.call-update
  242.8 24.7 %reduce-scatter.2.cloned.1.call-done = f32[768,96]{0,1:T(8,128)} async-done(((f32[768,384]{0,1:T(8,128)}), f32[768,96]{0,1:T(8,128)}) %reduce-scatter.2.cloned.1.call-update) | async-done | bytes 294928 | tf_op jit(solution)/shard_map/reduce_scatter | solution.py:33
  267.5 1.0 multiply_reduce_fusion
  268.5 0.0 copy-done.2
  268.6 0.6 fusion.2
  269.2 32.8 %psum.7 = f32[400]{0:T(512)} all-reduce(f32[400]{0:T(512)S(1)} %bitcast.26), channel_id=1, replica_groups=mesh['groups'=2,'ao'=4,'aux'=2,'occ'=2] {'ao','aux','occ'}, use_global_device_ids=true, to_apply=%region_2.0 | all-reduce | flops 400 | bytes 3200 | tf_op jit(solution)/shard_map/psum | solution.py:42
  (1 shorter events, 0.0 us)
Async XLA Ops:
  7.2 55.6 %all-gather.3.cloned.1.call-start = ((), (), s32[]{:S(2)}) async-start(), calls=%async_computation.2 | async-start | bytes 2949120 | tf_op jit(solution)/shard_map/all_gather | solution.py:10
  9.4 229.5 %all-gather.5.cloned.1.call-start = ((), (), s32[]{:S(2)}) async-start(), calls=%async_computation.3 | async-start | bytes 1843200 | tf_op jit(solution)/shard_map/all_gather | solution.py:28
  83.9 1.8 copy-start
  199.0 39.9 %copy-start.1 = (bf16[10,192,768]{2,1,0:T(8,128)(2,1)S(1)}, bf16[10,192,768]{2,1,0:T(8,128)(2,1)}, u32[]{:S(2)}) copy-start(bf16[10,192,768]{2,1,0:T(8,128)(2,1)} %copy-done) | copy-start | bytes 8847364
  204.2 64.3 %copy-start.2 = (s32[768]{0:T(1024)S(1)}, s32[768]{0:T(1024)}, u32[]{:S(2)}) copy-start(s32[768]{0:T(1024)} %param.5) | copy-start | bytes 9220
  204.3 63.2 %reduce-scatter.2.cloned.1.call-start = ((), (), s32[]{:S(2)}) async-start(), calls=%async_computation.4 | async-start | bytes 1474560 | tf_op jit(solution)/shard_map/reduce_scatter | solution.py:33
Sparse Core Ops, SparseCore 0:
  9.6 53.1 all-gather.2
  204.4 34.5 all-gather.4
  242.9 24.5 reduce-scatter.1
where the time goes:
time: 309 us
  blocking collectives  140 us (45%)
  waiting for transfers between devices  113 us (37%)
  matrix products  30.8 us (10%)
  between operations  13.8 us (4%)
  local copies, waits for them, and re-layouts  10 us (3%)
    all_to_all x1, blocking collectives, shards(): lax.all_to_all(half, 'ao', split_axis=1, concat_axis=2, tiled=True)  107 us
    all_gather x1, waiting for transfers between devices, shards(): coeff_all = lax.all_gather(coeffs, 'ao', axis=0, tiled=True)  53.3 us
    all_gather x1, waiting for transfers between devices, shards(): lax.all_gather(pair_block, 'ao', axis=1, tiled=True)  34.6 us
    psum x1, blocking collectives, shards(): atom_energy = lax.psum(atom_part, ('ao', 'aux', 'occ'))  32.8 us
    reduce_scatter x1, waiting for transfers between devices, shards(): lax.psum_scatter(accum_total * normalizer, ('aux', 'occ'), scatter_dimens...  24.7 us
    dot_general x1, matrix products, shards(): jnp.einsum('pmn,ni->pim', slab, own_cols, preferred_element_type=jnp.floa...  21.2 us
  transfers between devices with their start and end apart: 3, of which 3 were waited for; matrix products, arithmetic and copies ran while one was open for 0% of the time, Pallas kernels for 0%

commit v1 on v0

v1 whole, which is shorter than its diff:
```python
import functools

import jax
import jax.numpy as jnp
from jax import lax
from jax.experimental import pallas as pl
from jax.experimental.pallas import tpu as pltpu
from jax.sharding import PartitionSpec as P

NATOM = 400
MESH = pl.DeviceIdType.MESH
LAG = 2
SPLIT = 4


def kernel(
    dims, slab, coeffs, atom_of, grad_out, energy_out,
    slab_v, coeff_all, coeff_t, half, part, r_in, r_out, l_in, l_out, total, grad,
    sib, xout, xin, onehot, e_all,
    slab_sem, c_send_r, c_send_l, c_send_s, c_recv, c_recv_s,
    r_send, r_recv, l_send, l_recv, s_send, s_recv, x_send, x_recv, e_send, e_recv,
):
    n, nx, naux = dims
    rows, occ = coeffs.shape
    group_size = n * nx * 2
    chunks = naux * SPLIT
    height = occ // SPLIT
    width = occ // (nx * 2)
    z = lax.axis_index("ao")
    x = lax.axis_index("aux")
    c = lax.axis_index("occ")
    me = (z * nx + x) * 2 + c
    f32, bf16 = jnp.float32, jnp.bfloat16

    def slab_copy(p):
        return pltpu.make_async_copy(slab.at[c * naux + p], slab_v.at[p], slab_sem.at[p])

    for p in range(naux):
        slab_copy(p).start()

    barrier = pltpu.get_barrier_semaphore()

    def others(visit):
        def step(idx, carry):
            @pl.when(idx != me)
            def _():
                visit(idx, {"ao": idx // (nx * 2), "aux": (idx // 2) % nx, "occ": idx % 2})
            return carry
        lax.fori_loop(0, group_size, step, 0)

    others(lambda idx, dev: pl.semaphore_signal(barrier, inc=1, device_id=dev, device_id_type=MESH))
    pl.semaphore_wait(barrier, group_size - 1)

    def block(b, core):
        return coeff_all.at[pl.ds(pl.multiple_of(b * rows + core * (rows // 2), rows // 2), rows // 2)]

    def c_copy(b, dev, send, recv):
        return pltpu.make_async_remote_copy(
            src_ref=block(b, c), dst_ref=block(b, c), send_sem=send.at[b], recv_sem=recv.at[b],
            device_id=dev, device_id_type=MESH)

    def c_right(b):
        return c_copy(b, {"ao": z + 1}, c_send_r, c_recv)

    def c_left(b):
        return c_copy(b, {"ao": z - 1}, c_send_l, c_recv)

    def c_sib(b):
        return c_copy(b, {"occ": 1 - c}, c_send_s, c_recv_s)

    coeff_all[pl.ds(pl.multiple_of(z * rows, rows), rows), :] = coeffs[...]

    @pl.when(z + 1 < n)
    def _():
        c_right(z).start()

    @pl.when(z > 0)
    def _():
        c_left(z).start()

    coeff_t[...] = coeffs[...].astype(f32).T.astype(bf16)
    atoms = lax.broadcasted_iota(jnp.int32, (NATOM, rows), 0)
    onehot[...] = (atoms == atom_of[...]).astype(f32)
    grad[...] = jnp.zeros_like(grad)

    @pl.when(z == 0)
    def _():
        r_in[...] = jnp.zeros_like(r_in)

    @pl.when(z == n - 1)
    def _():
        l_in[...] = jnp.zeros_like(l_in)

    def gather_step(d, carry):
        @pl.when(z - d >= 0)
        def _():
            c_left(z - d).wait_recv()

            @pl.when(z + 1 < n)
            def _():
                c_right(z - d).start()
            c_sib(z - d).start()

        @pl.when(z + d < n)
        def _():
            c_right(z + d).wait_recv()

            @pl.when(z > 0)
            def _():
                c_left(z + d).start()
            c_sib(z + d).start()
        return carry

    lax.fori_loop(1, n, gather_step, 0)

    def gather_wait(b, carry):
        @pl.when(b != z)
        def _():
            pltpu.make_async_remote_copy(
                src_ref=block(b, 1 - c), dst_ref=block(b, 1 - c), send_sem=c_send_s.at[b],
                recv_sem=c_recv_s.at[b], device_id={"occ": 1 - c}, device_id_type=MESH).wait_recv()
        return carry

    lax.fori_loop(0, n, gather_wait, 0)

    mu = rows // 2

    def half_unit(p, unit):
        span = pl.ds(unit * mu, mu)
        half[p, span, :] = jnp.dot(
            slab_v[p, span, :], coeff_all[...], preferred_element_type=f32).astype(bf16)

    def part_unit(p):
        value = jnp.dot(coeff_t[...], half[p], preferred_element_type=f32)
        for k in range(SPLIT):
            part[p * SPLIT + k] = value[k * height:(k + 1) * height]

    def grad_unit(p):
        for k in range(SPLIT):
            grad[k * height:(k + 1) * height, :] += lax.dot_general(
                total[p * SPLIT + k], half[p], (((1,), (1,)), ((), ())), preferred_element_type=f32)

    def r_copy(i):
        return pltpu.make_async_remote_copy(
            src_ref=r_out.at[i], dst_ref=r_in.at[i], send_sem=r_send.at[i], recv_sem=r_recv.at[i],
            device_id={"ao": z + 1}, device_id_type=MESH)

    def l_copy(i):
        return pltpu.make_async_remote_copy(
            src_ref=l_out.at[i], dst_ref=l_in.at[i], send_sem=l_send.at[i], recv_sem=l_recv.at[i],
            device_id={"ao": z - 1}, device_id_type=MESH)

    def comm_slot(s):
        i_r = s - LAG * z
        i_l = s - LAG * (n - 1 - z)
        i_t = s - LAG * jnp.maximum(z, n - 1 - z)

        @pl.when((i_r >= 0) & (i_r < chunks))
        def _():
            @pl.when(z > 0)
            def _():
                r_copy(i_r).wait_recv()

            @pl.when(z + 1 < n)
            def _():
                r_out[i_r] = (part[i_r] + r_in[i_r].astype(f32)).astype(bf16)
                r_copy(i_r).start()

        @pl.when((i_l >= 0) & (i_l < chunks))
        def _():
            @pl.when(z + 1 < n)
            def _():
                l_copy(i_l).wait_recv()

            @pl.when(z > 0)
            def _():
                l_out[i_l] = (part[i_l] + l_in[i_l].astype(f32)).astype(bf16)
                l_copy(i_l).start()

        @pl.when((i_t >= 0) & (i_t < chunks))
        def _():
            total[i_t] = (
                part[i_t] + r_in[i_t].astype(f32) + l_in[i_t].astype(f32)).astype(bf16)

    slab_copy(0).wait()
    half_unit(0, 0)
    half_unit(0, 1)
    part_unit(0)

    delay = -(-LAG * (n - 1) // SPLIT)

    def group(g, carry):
        for k in range(SPLIT):
            comm_slot(g * SPLIT + k)
            if k < 3:
                @pl.when(g + 1 < naux)
                def _():
                    if k == 0:
                        slab_copy(g + 1).wait()
                    if k < 2:
                        half_unit(g + 1, k)
                    else:
                        part_unit(g + 1)
            else:
                @pl.when(g >= delay)
                def _():
                    grad_unit(g - delay)
        return carry

    lax.fori_loop(0, naux + delay, group, 0)

    def rows_of(x_to, core):
        return pl.ds(pl.multiple_of((x_to * 2 + core) * width, width), width)

    def s_copy(x_to):
        return pltpu.make_async_remote_copy(
            src_ref=grad.at[rows_of(x_to, 1 - c)], dst_ref=sib.at[x_to], send_sem=s_send.at[x_to],
            recv_sem=s_recv.at[x_to], device_id={"occ": 1 - c}, device_id_type=MESH)

    def x_copy(d):
        return pltpu.make_async_remote_copy(
            src_ref=xout.at[d - 1], dst_ref=xin.at[d - 1], send_sem=x_send.at[d - 1],
            recv_sem=x_recv.at[d - 1], device_id={"aux": lax.rem(x + d, nx)}, device_id_type=MESH)

    for d in range(1, nx + 1):
        s_copy(lax.rem(x + d, nx)).start()
    for d in range(1, nx + 1):
        x_to = lax.rem(x + d, nx)
        s_copy(x_to).wait_recv()
        both = grad[rows_of(x_to, c), :] + sib[x_to]
        if d < nx:
            xout[d - 1] = both.astype(bf16)
            x_copy(d).start()
    for d in range(1, nx):
        x_copy(d).wait_recv()
        both = both + xin[d - 1].astype(f32)
    normalizer = 1.0 / jnp.sqrt(jnp.float32(naux * 2 * nx * occ))
    both = both * normalizer
    grad_out[...] = both

    weighted = jnp.sum(coeff_t[rows_of(x, c), :].astype(f32) * both, axis=0, keepdims=True)
    e_all[me] = lax.dot_general(
        jnp.broadcast_to(weighted, (8, rows)), onehot[...], (((1,), (1,)), ((), ())),
        precision=lax.Precision.HIGHEST, preferred_element_type=f32)

    def e_copy(slot, peer, dev):
        return pltpu.make_async_remote_copy(
            src_ref=e_all.at[slot], dst_ref=e_all.at[slot], send_sem=e_send.at[peer],
            recv_sem=e_recv.at[slot], device_id=dev, device_id_type=MESH)

    others(lambda idx, dev: e_copy(me, idx, dev).start())

    def sent(i, carry):
        @pl.when(z + 1 < n)
        def _():
            r_copy(i).wait_send()

        @pl.when(z > 0)
        def _():
            l_copy(i).wait_send()
        return carry

    lax.fori_loop(0, chunks, sent, 0)

    def c_sent(b, carry):
        @pl.when((b <= z) & (z + 1 < n))
        def _():
            c_right(b).wait_send()

        @pl.when((b >= z) & (z > 0))
        def _():
            c_left(b).wait_send()

        @pl.when(b != z)
        def _():
            c_sib(b).wait_send()
        return carry

    lax.fori_loop(0, n, c_sent, 0)
    for d in range(1, nx + 1):
        s_copy(lax.rem(x + d, nx)).wait_send()
    for d in range(1, nx):
        x_copy(d).wait_send()
    others(lambda idx, dev: e_copy(idx, idx, dev).wait_recv())
    others(lambda idx, dev: e_copy(me, idx, dev).wait_send())
    energy_out[...] = lax.fori_loop(
        1, group_size, lambda i, acc: acc + e_all[i], e_all[0])


def shards(n, nx, slab, coeffs, atom_of):
    naux = slab.shape[0] // 2
    rows, occ = coeffs.shape
    nu = slab.shape[2]
    chunks, height, width = naux * SPLIT, occ // SPLIT, occ // (nx * 2)
    group_size = n * nx * 2
    bf16, f32 = jnp.bfloat16, jnp.float32
    dma = lambda k: pltpu.SemaphoreType.DMA((k,))
    vmem = pl.BlockSpec(memory_space=pltpu.VMEM)
    chunk = pltpu.VMEM((chunks, height, occ), bf16)
    macs = naux * rows * occ * (nu + 2 * occ)
    grad_t, energy = pl.pallas_call(
        functools.partial(kernel, (n, nx, naux)),
        out_shape=(
            jax.ShapeDtypeStruct((width, rows), f32),
            jax.ShapeDtypeStruct((8, NATOM), f32),
        ),
        in_specs=[pl.BlockSpec(memory_space=pl.ANY), vmem, vmem],
        out_specs=(vmem, vmem),
        scratch_shapes=[
            pltpu.VMEM((naux, rows, nu), bf16),
            pltpu.VMEM((nu, occ), bf16),
            pltpu.VMEM((occ, rows), bf16),
            pltpu.VMEM((naux, rows, occ), bf16),
            pltpu.VMEM((chunks, height, occ), f32),
            chunk, chunk, chunk, chunk, chunk,
            pltpu.VMEM((occ, rows), f32),
            pltpu.VMEM((nx, width, rows), f32),
            pltpu.VMEM((nx - 1, width, rows), bf16),
            pltpu.VMEM((nx - 1, width, rows), bf16),
            pltpu.VMEM((NATOM, rows), f32),
            pltpu.VMEM((group_size, 8, NATOM), f32),
            dma(naux), dma(n), dma(n), dma(n), dma(n), dma(n),
            dma(chunks), dma(chunks), dma(chunks), dma(chunks),
            dma(nx), dma(nx), dma(nx - 1), dma(nx - 1), dma(group_size), dma(group_size),
        ],
        compiler_params=pltpu.CompilerParams(
            collective_id=0, has_side_effects=True, vmem_limit_bytes=56 * 1024 * 1024),
        cost_estimate=pl.CostEstimate(
            flops=2 * macs, bytes_accessed=naux * rows * nu * 2, transcendentals=0),
    )(slab, coeffs, atom_of.reshape(1, rows))
    return grad_t.T, energy[0]


def solution(mesh):
    in_specs = (P(("groups", "aux"), "ao", None), P(("groups", "ao"), None), P(("groups", "ao")))
    out_specs = (P(("groups", "ao"), ("aux", "occ")), P("groups"))
    body = functools.partial(shards, mesh.shape["ao"], mesh.shape["aux"])
    return jax.shard_map(body, mesh=mesh, in_specs=in_specs, out_specs=out_specs, check_vma=False)
```

time: 309 us -> 97 us (0.31)
  blocking collectives: 140 us -> 0 us
  waiting for transfers between devices: 113 us -> 0 us
  Pallas kernels: 0 us -> 91.6 us
  matrix products: 30.8 us -> 0 us
  between operations: 13.8 us -> 0.64 us
  local copies, waits for them, and re-layouts: 10 us -> 4.26 us
    all_to_all x1 -> x0, blocking collectives: 107 us -> none  [shards(): lax.all_to_all(half, 'ao', split_axis=1, concat_axis=2, tiled=True)]
    pallas_call x0 -> x1, Pallas kernels: none -> 91.6 us  [shards(): pl.pallas_call(functools.partial(kernel, (n, nx, naux)), out_shape=(jax.S...]
    all_gather x2 -> x0, waiting for transfers between devices: 87.9 us -> none  [the longest x1 53.3 us: shards(): coeff_all = lax.all_gather(coeffs, 'ao', axis=0, tiled=True)]
    psum x1 -> x0, blocking collectives: 32.8 us -> none  [shards(): atom_energy = lax.psum(atom_part, ('ao', 'aux', 'occ'))]
    dot_general x4 -> x0, matrix products: 30.8 us -> none  [the longest x1 21.2 us: shards(): jnp.einsum('pmn,ni->pim', slab, own_cols, preferred_element_type=jnp.floa...]
    reduce_scatter x1 -> x0, waiting for transfers between devices: 24.7 us -> none  [shards(): lax.psum_scatter(accum_total * normalizer, ('aux', 'occ'), scatter_dimens...]
    all_to_all x2 -> x0, local copies, waits for them, and re-layouts: 6.07 us -> none  [shards(): lax.all_to_all(half, 'ao', split_axis=1, concat_axis=2, tiled=True)]
  transfers between devices with their start and end apart: 3 -> 0, of which waited for: 3 -> 0; matrix products, arithmetic and copies ran while one was open for 0% -> 0% of each run, Pallas kernels for 0% -> 0%
where the time goes in v1:
time: 97 us; the launch traced here: 96.5 us
  Pallas kernels  91.6 us (94%)
  local copies, waits for them, and re-layouts  4.26 us (4%)
    pallas_call x1, Pallas kernels, shards(): pl.pallas_call(functools.partial(kernel, (n, nx, naux)), out_shape=(jax.S...  91.6 us

profile of v1, /device:TPU:0, one launch (start us, length us, event | category | flops | bytes accessed | tf_op | source)
XLA Modules:
  0.0 96.5 jit_solution(8008208656279162463)
XLA Ops:
  0.6 1.3 %reshape.7.atom_of = s32[1,768]{1,0:T(1,128)} reshape(s32[768]{0:T(1024)} %param.5) | data formatting | bytes 6144 | tf_op jit(solution)/shard_map/reshape | solution.py:330
  1.9 91.6 %shard_map.50 = (f32[96,768]{1,0:T(8,128)}, f32[8,400]{1,0:T(8,128)}) custom-call(bf16[10,768,3072]{2,1,0:T(8,128)(2,1)} %slab.1, bf16[768,384]{1,0:T(8,128)(2,1)} %coeffs.1, s32[1,768]{1,0:T(1,128)} %reshape.7.atom_of), custom_call_target="tpu_custom_call" | custom-call | flops 11324620800 | bytes 23592960 | tf_op jit(solution)/shard_map/pallas_call | solution.py:301
  93.5 1.3 %slice.3 = f32[1,400]{1,0:T(1,128)} slice(f32[8,400]{1,0:T(8,128)} %get-tuple-element.5), slice={[0:1], [0:400]} | slice | bytes 3200 | tf_op jit(solution)/shard_map/slice | solution.py:331
  94.8 1.7 %copy.6 = f32[768,96]{0,1:T(8,128)} copy(f32[768,96]{0,1:T(8,128)} %bitcast.2) | data formatting | bytes 589824

commit v2 on v1

v2 whole, which is shorter than its diff:
```python
import functools

import jax
import jax.numpy as jnp
from jax import lax
from jax.experimental import pallas as pl
from jax.experimental.pallas import tpu as pltpu
from jax.sharding import PartitionSpec as P

NATOM = 400
MESH = pl.DeviceIdType.MESH
LAG = 2
SPLIT = 3


def kernel(
    dims, slab, coeffs, atom_of, grad_out, energy_out,
    slab_v, coeff_all, coeff_t, half, part, r_in, r_out, l_in, l_out, total, grad,
    sib, xout, xin, onehot, e_all, w_sum,
    slab_sem, c_send_r, c_send_l, c_recv, c_send_s, c_recv_s, c_send_x, c_recv_x,
    r_send, r_recv, l_send, l_recv, s_send, s_recv, x_send, x_recv, e_send, e_recv,
):
    n, nx, naux, share = dims
    rows, occ = coeffs.shape
    group_size = n * nx * 2
    chunks = naux * SPLIT
    height = occ // SPLIT
    width = occ // (nx * 2)
    third = width // SPLIT
    piece = rows // (2 * share)
    z = lax.axis_index("ao")
    x = lax.axis_index("aux")
    c = lax.axis_index("occ")
    me = (z * nx + x) * 2 + c
    f32, bf16 = jnp.float32, jnp.bfloat16

    def slab_copy(p):
        return pltpu.make_async_copy(slab.at[c * naux + p], slab_v.at[p], slab_sem.at[p])

    for p in range(naux):
        slab_copy(p).start()

    barrier = pltpu.get_barrier_semaphore()

    def others(visit):
        def step(idx, carry):
            @pl.when(idx != me)
            def _():
                visit(idx, {"ao": idx // (nx * 2), "aux": (idx // 2) % nx, "occ": idx % 2})
            return carry
        lax.fori_loop(0, group_size, step, 0)

    others(lambda idx, dev: pl.semaphore_signal(barrier, inc=1, device_id=dev, device_id_type=MESH))
    pl.semaphore_wait(barrier, group_size - 1)

    xi = x if share > 1 else 0

    def c_copy(b, xx, dev, send, recv):
        ref = coeff_all.at[pl.ds(pl.multiple_of(b * rows + (xx * 2 + c) * piece, piece), piece)]
        return pltpu.make_async_remote_copy(
            src_ref=ref, dst_ref=ref, send_sem=send, recv_sem=recv, device_id=dev, device_id_type=MESH)

    def c_right(b):
        return c_copy(b, xi, {"ao": z + 1}, c_send_r.at[b], c_recv.at[b])

    def c_left(b):
        return c_copy(b, xi, {"ao": z - 1}, c_send_l.at[b], c_recv.at[b])

    def c_sib(b, xx):
        return c_copy(b, xx, {"occ": 1 - c}, c_send_s.at[b, xx], c_recv_s.at[b, xx])

    def c_across(b, d):
        return c_copy(b, xi, {"aux": lax.rem(x + d, nx)}, c_send_x.at[b, d], c_recv_x.at[b, xi])

    coeff_all[pl.ds(pl.multiple_of(z * rows, rows), rows), :] = coeffs[...]

    @pl.when(z + 1 < n)
    def _():
        c_right(z).start()

    @pl.when(z > 0)
    def _():
        c_left(z).start()

    turned = coeffs[...].astype(f32).T
    for k in range(SPLIT):
        for q in range(2 * nx):
            first = q * width + k * third
            coeff_t[k * height + q * third:k * height + (q + 1) * third, :] = (
                turned[first:first + third].astype(bf16))
    atoms = lax.broadcasted_iota(jnp.int32, (NATOM, rows), 0)
    onehot[...] = (atoms == atom_of[...].reshape(1, rows)).astype(f32)
    grad[...] = jnp.zeros_like(grad)

    @pl.when(z == 0)
    def _():
        r_in[...] = jnp.zeros_like(r_in)

    @pl.when(z == n - 1)
    def _():
        l_in[...] = jnp.zeros_like(l_in)

    def gather_step(d, carry):
        @pl.when((z - d >= 0) & (d < n))
        def _():
            b = z - d
            c_left(b).wait_recv()

            @pl.when(z + 1 < n)
            def _():
                c_right(b).start()
            for dx in range(1, share):
                c_across(b, dx).start()
            c_sib(b, xi).start()

        @pl.when((z + d < n) & (d < n))
        def _():
            b = z + d
            c_right(b).wait_recv()

            @pl.when(z > 0)
            def _():
                c_left(b).start()
            for dx in range(1, share):
                c_across(b, dx).start()
            c_sib(b, xi).start()

        def pass_on(b):
            for dx in range(1, share):
                xx = lax.rem(x + dx, nx)
                ref = coeff_all.at[pl.ds(pl.multiple_of(b * rows + (xx * 2 + c) * piece, piece), piece)]
                pltpu.make_async_remote_copy(
                    src_ref=ref, dst_ref=ref, send_sem=c_send_x.at[b, dx], recv_sem=c_recv_x.at[b, xx],
                    device_id={"aux": xx}, device_id_type=MESH).wait_recv()
                c_sib(b, xx).start()

        @pl.when((d > 1) & (z - d + 1 >= 0))
        def _():
            pass_on(z - d + 1)

        @pl.when((d > 1) & (z + d - 1 < n))
        def _():
            pass_on(z + d - 1)
        return carry

    lax.fori_loop(1, n + 1, gather_step, 0)

    def gather_wait(b, carry):
        @pl.when(b != z)
        def _():
            for xx in range(share):
                ref = coeff_all.at[
                    pl.ds(pl.multiple_of(b * rows + (xx * 2 + 1 - c) * piece, piece), piece)]
                pltpu.make_async_remote_copy(
                    src_ref=ref, dst_ref=ref, send_sem=c_send_s.at[b, xx], recv_sem=c_recv_s.at[b, xx],
                    device_id={"occ": 1 - c}, device_id_type=MESH).wait_recv()
        return carry

    lax.fori_loop(0, n, gather_wait, 0)

    mu = rows // 2

    def half_unit(p, unit):
        span = pl.ds(unit * mu, mu)
        half[p, span, :] = jnp.dot(
            slab_v[p, span, :], coeff_all[...], preferred_element_type=f32).astype(bf16)

    def part_unit(p):
        value = jnp.dot(coeff_t[...], half[p], preferred_element_type=f32)
        for k in range(SPLIT - 1):
            part[p * (SPLIT - 1) + k] = value[k * height:(k + 1) * height]
        part[naux * (SPLIT - 1) + p] = value[(SPLIT - 1) * height:]

    def grad_unit(p, k, i):
        grad[k] += lax.dot_general(
            total[i], half[p], (((1,), (1,)), ((), ())), preferred_element_type=f32)

    def rows_of(x_to, core):
        return pl.ds(pl.multiple_of((x_to * 2 + core) * third, third), third)

    def s_copy(k, x_to):
        return pltpu.make_async_remote_copy(
            src_ref=grad.at[k, rows_of(x_to, 1 - c)], dst_ref=sib.at[k, x_to],
            send_sem=s_send.at[k, x_to], recv_sem=s_recv.at[k, x_to], device_id={"occ": 1 - c},
            device_id_type=MESH)

    def x_copy(k, d):
        return pltpu.make_async_remote_copy(
            src_ref=xout.at[k, d], dst_ref=xin.at[k, d], send_sem=x_send.at[k, d],
            recv_sem=x_recv.at[k, d], device_id={"aux": lax.rem(x + d, nx)}, device_id_type=MESH)

    normalizer = 1.0 / jnp.sqrt(jnp.float32(naux * 2 * nx * occ))

    def across_cores(ks):
        for d in range(1, nx + 1):
            for k in ks:
                s_copy(k, lax.rem(x + d, nx)).start()

    def across_aux(ks):
        for d in range(1, nx + 1):
            x_to = lax.rem(x + d, nx)
            for k in ks:
                s_copy(k, x_to).wait_recv()
                both = grad[k, rows_of(x_to, c), :] + sib[k, x_to]
                if d < nx:
                    xout[k, d] = both.astype(bf16)
                    x_copy(k, d).start()
                else:
                    grad_out[k * third:(k + 1) * third, :] = both

    def finish(ks):
        for k in ks:
            span = slice(k * third, (k + 1) * third)
            both = grad_out[span, :]
            for d in range(1, nx):
                x_copy(k, d).wait_recv()
                both = both + xin[k, d].astype(f32)
            grad_out[span, :] = both * normalizer

    def weigh(k):
        value = coeff_t[k * height:(k + 1) * height, :].astype(f32) * grad[k]
        return jnp.sum(value, axis=0, keepdims=True)

    def r_copy(i):
        return pltpu.make_async_remote_copy(
            src_ref=r_out.at[i], dst_ref=r_in.at[i], send_sem=r_send.at[i], recv_sem=r_recv.at[i],
            device_id={"ao": z + 1}, device_id_type=MESH)

    def l_copy(i):
        return pltpu.make_async_remote_copy(
            src_ref=l_out.at[i], dst_ref=l_in.at[i], send_sem=l_send.at[i], recv_sem=l_recv.at[i],
            device_id={"ao": z - 1}, device_id_type=MESH)

    def comm_slot(s):
        i_r = s - LAG * z
        i_l = s - LAG * (n - 1 - z)
        i_t = s - LAG * jnp.maximum(z, n - 1 - z)

        @pl.when((i_r >= 0) & (i_r < chunks))
        def _():
            @pl.when(z > 0)
            def _():
                r_copy(i_r).wait_recv()

            @pl.when(z + 1 < n)
            def _():
                r_out[i_r] = (part[i_r] + r_in[i_r].astype(f32)).astype(bf16)
                r_copy(i_r).start()

        @pl.when((i_l >= 0) & (i_l < chunks))
        def _():
            @pl.when(z + 1 < n)
            def _():
                l_copy(i_l).wait_recv()

            @pl.when(z > 0)
            def _():
                l_out[i_l] = (part[i_l] + l_in[i_l].astype(f32)).astype(bf16)
                l_copy(i_l).start()

        @pl.when((i_t >= 0) & (i_t < chunks))
        def _():
            total[i_t] = (
                part[i_t] + r_in[i_t].astype(f32) + l_in[i_t].astype(f32)).astype(bf16)

    slab_copy(0).wait()
    half_unit(0, 0)
    half_unit(0, 1)
    part_unit(0)

    early = SPLIT - 1
    reach = LAG * (n - 1)
    done = early * (naux - 1) + reach + early - 1

    def slot(s, carry):
        comm_slot(s)
        p = s // early + 1
        for k in range(early):
            @pl.when((p < naux) & (lax.rem(s, early) == k))
            def _():
                if k == 0:
                    slab_copy(p).wait()
                    half_unit(p, 0)
                if k == 1:
                    half_unit(p, 1)
                if k == early - 1:
                    part_unit(p)
        t = s - reach - early + 1

        @pl.when((t >= 0) & (t <= early * (naux - 1)) & (lax.rem(t + early * n, early) == 0))
        def _():
            for k in range(early):
                grad_unit(t // early, k, t + k)

        @pl.when(s > done)
        def _():
            grad_unit(s - done - 1, early, early * naux + s - done - 1)

        @pl.when(s == done)
        def _():
            across_cores(range(early))

        @pl.when(s == done + 1)
        def _():
            w_sum[...] = sum(weigh(k) for k in range(early))

        @pl.when(s == done + 2)
        def _():
            across_aux(range(early))

        @pl.when(s == done + 4)
        def _():
            finish(range(early))
        return carry

    lax.fori_loop(0, chunks + reach, slot, 0)
    across_cores([early])

    weighted = (w_sum[...] + weigh(early)) * normalizer
    e_all[me] = lax.dot_general(
        jnp.broadcast_to(weighted, (8, rows)), onehot[...], (((1,), (1,)), ((), ())),
        precision=lax.Precision.HIGHEST, preferred_element_type=f32)

    def e_copy(slot, peer, dev):
        return pltpu.make_async_remote_copy(
            src_ref=e_all.at[slot], dst_ref=e_all.at[slot], send_sem=e_send.at[peer],
            recv_sem=e_recv.at[slot], device_id=dev, device_id_type=MESH)

    others(lambda idx, dev: e_copy(me, idx, dev).start())

    across_aux([early])
    finish([early])

    def sent(i, carry):
        @pl.when(z + 1 < n)
        def _():
            r_copy(i).wait_send()

        @pl.when(z > 0)
        def _():
            l_copy(i).wait_send()
        return carry

    lax.fori_loop(0, chunks, sent, 0)

    def c_sent(b, carry):
        @pl.when((b <= z) & (z + 1 < n))
        def _():
            c_right(b).wait_send()

        @pl.when((b >= z) & (z > 0))
        def _():
            c_left(b).wait_send()

        @pl.when(b != z)
        def _():
            for xx in range(share):
                c_sib(b, xx).wait_send()
            for dx in range(1, share):
                c_across(b, dx).wait_send()
        return carry

    lax.fori_loop(0, n, c_sent, 0)
    for k in range(SPLIT):
        for d in range(1, nx + 1):
            s_copy(k, lax.rem(x + d, nx)).wait_send()
        for d in range(1, nx):
            x_copy(k, d).wait_send()
    others(lambda idx, dev: e_copy(idx, idx, dev).wait_recv())
    others(lambda idx, dev: e_copy(me, idx, dev).wait_send())
    energy_out[...] = lax.fori_loop(
        1, group_size, lambda i, acc: acc + e_all[i], e_all[0])[0]


def shards(n, nx, slab, coeffs, atom_of):
    naux = slab.shape[0] // 2
    rows, occ = coeffs.shape
    nu = slab.shape[2]
    chunks, height, width = naux * SPLIT, occ // SPLIT, occ // (nx * 2)
    group_size = n * nx * 2
    bf16, f32 = jnp.bfloat16, jnp.float32
    third = width // SPLIT
    share = nx if rows % (32 * nx) == 0 else 1
    dma = lambda *k: pltpu.SemaphoreType.DMA(k)
    vmem = pl.BlockSpec(memory_space=pltpu.VMEM)
    chunk = pltpu.VMEM((chunks, height, occ), bf16)
    macs = naux * rows * occ * (nu + 2 * occ)
    grad_t, energy = pl.pallas_call(
        functools.partial(kernel, (n, nx, naux, share)),
        out_shape=(
            jax.ShapeDtypeStruct((width, rows), f32),
            jax.ShapeDtypeStruct((NATOM,), f32),
        ),
        in_specs=[pl.BlockSpec(memory_space=pl.ANY), vmem, vmem],
        out_specs=(vmem, vmem),
        scratch_shapes=[
            pltpu.VMEM((naux, rows, nu), bf16),
            pltpu.VMEM((nu, occ), bf16),
            pltpu.VMEM((occ, rows), bf16),
            pltpu.VMEM((naux, rows, occ), bf16),
            pltpu.VMEM((chunks, height, occ), f32),
            chunk, chunk, chunk, chunk, chunk,
            pltpu.VMEM((SPLIT, height, rows), f32),
            pltpu.VMEM((SPLIT, nx, third, rows), f32),
            pltpu.VMEM((SPLIT, nx, third, rows), bf16),
            pltpu.VMEM((SPLIT, nx, third, rows), bf16),
            pltpu.VMEM((NATOM, rows), f32),
            pltpu.VMEM((group_size, 8, NATOM), f32),
            pltpu.VMEM((1, rows), f32),
            dma(naux), dma(n), dma(n), dma(n),
            dma(n, share), dma(n, share), dma(n, share), dma(n, share),
            dma(chunks), dma(chunks), dma(chunks), dma(chunks),
            dma(SPLIT, nx), dma(SPLIT, nx), dma(SPLIT, nx), dma(SPLIT, nx), dma(group_size), dma(group_size),
        ],
        compiler_params=pltpu.CompilerParams(
            collective_id=0, has_side_effects=True, vmem_limit_bytes=56 * 1024 * 1024),
        cost_estimate=pl.CostEstimate(
            flops=2 * macs, bytes_accessed=naux * rows * nu * 2, transcendentals=0),
    )(slab, coeffs, atom_of)
    return grad_t.T, energy


def solution(mesh):
    in_specs = (P(("groups", "aux"), "ao", None), P(("groups", "ao"), None), P(("groups", "ao")))
    out_specs = (P(("groups", "ao"), ("aux", "occ")), P("groups"))
    body = functools.partial(shards, mesh.shape["ao"], mesh.shape["aux"])
    return jax.shard_map(body, mesh=mesh, in_specs=in_specs, out_specs=out_specs, check_vma=False)
```

time: 97 us -> 84.1 us (0.87)
  Pallas kernels: 91.6 us -> 80.3 us
  local copies, waits for them, and re-layouts: 4.26 us -> 2.95 us
    pallas_call x1, Pallas kernels: 91.6 us -> 80.3 us  [shards(): pl.pallas_call(functools.partial(kernel, (n, nx, naux, share)), out_shape...]
    slice x1 -> x0, local copies, waits for them, and re-layouts: 1.3 us -> none  [shards(): return (grad_t.T, energy[0])]
    reshape x1 -> x0, local copies, waits for them, and re-layouts: 1.27 us -> none  [shards(): atom_of.reshape(1, rows)]
    unnamed x1 -> x2, local copies, waits for them, and re-layouts: 1.69 us -> 2.95 us
where the time goes in v2:
time: 84.1 us; the launch traced here: 83.9 us
  Pallas kernels  80.3 us (95%)
  local copies, waits for them, and re-layouts  2.95 us (4%)
    pallas_call x1, Pallas kernels, shards(): pl.pallas_call(functools.partial(kernel, (n, nx, naux, share)), out_shape...  80.3 us
    unnamed x2, local copies, waits for them, and re-layouts  2.95 us

profile of v2, /device:TPU:0, one launch (start us, length us, event | category | flops | bytes accessed | tf_op | source)
XLA Modules:
  0.0 83.9 jit_solution(10261126279218866183)
XLA Ops:
  0.6 80.3 %shard_map.50 = (f32[96,768]{1,0:T(8,128)}, f32[400]{0:T(512)}) custom-call(bf16[10,768,3072]{2,1,0:T(8,128)(2,1)} %slab.1, bf16[768,384]{1,0:T(8,128)(2,1)} %coeffs.1, s32[768]{0:T(1024)} %atom_of.1), custom_call_target="tpu_custom_call" | custom-call | flops 11324620800 | bytes 23592960 | tf_op jit(solution)/shard_map/pallas_call | solution.py:388
  80.9 1.7 %copy.7 = f32[768,96]{0,1:T(8,128)} copy(f32[768,96]{0,1:T(8,128)} %bitcast.1) | data formatting | bytes 589824
  82.6 1.3 %copy.8 = f32[400]{0:T(512)} copy(f32[400]{0:T(512)} %get-tuple-element.9) | data formatting | bytes 3200

commit v3 on v2

--- a/solution.py
+++ b/solution.py
@@ -12,17 +12,18 @@
 LAG = 2
 SPLIT = 3
 
+PIECES = 1
+
 
 def kernel(
     dims, slab, coeffs, atom_of, grad_out, energy_out,
     slab_v, coeff_all, coeff_t, half, part, r_in, r_out, l_in, l_out, total, grad,
-    sib, xout, xin, onehot, e_all, w_sum,
+    sib, xout, xin, onehot, e_s, e_x, e_z, w_sum, acc,
     slab_sem, c_send_r, c_send_l, c_recv, c_send_s, c_recv_s, c_send_x, c_recv_x,
-    r_send, r_recv, l_send, l_recv, s_send, s_recv, x_send, x_recv, e_send, e_recv,
+    r_send, r_recv, l_send, l_recv, s_send, s_recv, x_send, x_recv, es_send, es_recv, ex_send, ex_recv, ez_send, ez_recv,
 ):
     n, nx, naux, share = dims
     rows, occ = coeffs.shape
-    group_size = n * nx * 2
     chunks = naux * SPLIT
     height = occ // SPLIT
     width = occ // (nx * 2)
@@ -31,7 +32,6 @@
     z = lax.axis_index("ao")
     x = lax.axis_index("aux")
     c = lax.axis_index("occ")
-    me = (z * nx + x) * 2 + c
     f32, bf16 = jnp.float32, jnp.bfloat16
 
     def slab_copy(p):
@@ -42,16 +42,22 @@
 
     barrier = pltpu.get_barrier_semaphore()
 
-    def others(visit):
+    def along_ao(visit):
         def step(idx, carry):
-            @pl.when(idx != me)
-            def _():
-                visit(idx, {"ao": idx // (nx * 2), "aux": (idx // 2) % nx, "occ": idx % 2})
+            @pl.when(idx != z)
+            def _():
+                visit(idx, {"ao": idx})
             return carry
-        lax.fori_loop(0, group_size, step, 0)
-
-    others(lambda idx, dev: pl.semaphore_signal(barrier, inc=1, device_id=dev, device_id_type=MESH))
-    pl.semaphore_wait(barrier, group_size - 1)
+        lax.fori_loop(0, n, step, 0)
+
+    def greet(dev):
+        pl.semaphore_signal(barrier, inc=1, device_id=dev, device_id_type=MESH)
+
+    along_ao(lambda idx, dev: greet(dev))
+    greet({"occ": 1 - c})
+    for d in range(1, nx):
+        greet({"aux": lax.rem(x + d, nx)})
+    pl.semaphore_wait(barrier, n - 1 + nx)
 
     xi = x if share > 1 else 0
 
@@ -143,20 +149,36 @@
             pass_on(z + d - 1)
         return carry
 
-    lax.fori_loop(1, n + 1, gather_step, 0)
-
-    def gather_wait(b, carry):
-        @pl.when(b != z)
-        def _():
-            for xx in range(share):
-                ref = coeff_all.at[
-                    pl.ds(pl.multiple_of(b * rows + (xx * 2 + 1 - c) * piece, piece), piece)]
-                pltpu.make_async_remote_copy(
-                    src_ref=ref, dst_ref=ref, send_sem=c_send_s.at[b, xx], recv_sem=c_recv_s.at[b, xx],
-                    device_id={"occ": 1 - c}, device_id_type=MESH).wait_recv()
+    def arrived(b):
+        for xx in range(share):
+            ref = coeff_all.at[
+                pl.ds(pl.multiple_of(b * rows + (xx * 2 + 1 - c) * piece, piece), piece)]
+            pltpu.make_async_remote_copy(
+                src_ref=ref, dst_ref=ref, send_sem=c_send_s.at[b, xx], recv_sem=c_recv_s.at[b, xx],
+                device_id={"occ": 1 - c}, device_id_type=MESH).wait_recv()
+
+    by_block = rows % 128 == 0
+
+    def consume(b):
+        if by_block:
+            span = pl.ds(pl.multiple_of(b * rows, rows), rows)
+            acc[...] += jnp.dot(
+                slab_v[0, :, span], coeff_all[span, :], preferred_element_type=f32)
+
+    slab_copy(0).wait()
+    acc[...] = jnp.zeros_like(acc)
+    consume(z)
+
+    def gather_and_use(d, carry):
+        gather_step(d, carry)
+        for b, there in ((z - d + 1, z - d + 1 >= 0), (z + d - 1, z + d - 1 < n)):
+            @pl.when((d > 1) & there)
+            def _():
+                arrived(b)
+                consume(b)
         return carry
 
-    lax.fori_loop(0, n, gather_wait, 0)
+    lax.fori_loop(1, n + 1, gather_and_use, 0)
 
     mu = rows // 2
 
@@ -221,51 +243,59 @@
         value = coeff_t[k * height:(k + 1) * height, :].astype(f32) * grad[k]
         return jnp.sum(value, axis=0, keepdims=True)
 
-    def r_copy(i):
-        return pltpu.make_async_remote_copy(
-            src_ref=r_out.at[i], dst_ref=r_in.at[i], send_sem=r_send.at[i], recv_sem=r_recv.at[i],
+    low = height // PIECES
+
+    def r_copy(i, h):
+        return pltpu.make_async_remote_copy(
+            src_ref=r_out.at[i, pl.ds(h * low, low)], dst_ref=r_in.at[i, pl.ds(h * low, low)],
+            send_sem=r_send.at[i, h], recv_sem=r_recv.at[i, h],
             device_id={"ao": z + 1}, device_id_type=MESH)
 
-    def l_copy(i):
-        return pltpu.make_async_remote_copy(
-            src_ref=l_out.at[i], dst_ref=l_in.at[i], send_sem=l_send.at[i], recv_sem=l_recv.at[i],
+    def l_copy(i, h):
+        return pltpu.make_async_remote_copy(
+            src_ref=l_out.at[i, pl.ds(h * low, low)], dst_ref=l_in.at[i, pl.ds(h * low, low)],
+            send_sem=l_send.at[i, h], recv_sem=l_recv.at[i, h],
             device_id={"ao": z - 1}, device_id_type=MESH)
 
     def comm_slot(s):
         i_r = s - LAG * z
         i_l = s - LAG * (n - 1 - z)
         i_t = s - LAG * jnp.maximum(z, n - 1 - z)
-
-        @pl.when((i_r >= 0) & (i_r < chunks))
-        def _():
-            @pl.when(z > 0)
-            def _():
-                r_copy(i_r).wait_recv()
-
-            @pl.when(z + 1 < n)
-            def _():
-                r_out[i_r] = (part[i_r] + r_in[i_r].astype(f32)).astype(bf16)
-                r_copy(i_r).start()
-
-        @pl.when((i_l >= 0) & (i_l < chunks))
-        def _():
-            @pl.when(z + 1 < n)
-            def _():
-                l_copy(i_l).wait_recv()
-
-            @pl.when(z > 0)
-            def _():
-                l_out[i_l] = (part[i_l] + l_in[i_l].astype(f32)).astype(bf16)
-                l_copy(i_l).start()
+        for h in range(PIECES):
+            span = pl.ds(h * low, low)
+
+            @pl.when((i_r >= 0) & (i_r < chunks))
+            def _():
+                @pl.when(z > 0)
+                def _():
+                    r_copy(i_r, h).wait_recv()
+
+                @pl.when(z + 1 < n)
+                def _():
+                    r_out[i_r, span] = (part[i_r, span] + r_in[i_r, span].astype(f32)).astype(bf16)
+                    r_copy(i_r, h).start()
+
+            @pl.when((i_l >= 0) & (i_l < chunks))
+            def _():
+                @pl.when(z + 1 < n)
+                def _():
+                    l_copy(i_l, h).wait_recv()
+
+                @pl.when(z > 0)
+                def _():
+                    l_out[i_l, span] = (part[i_l, span] + l_in[i_l, span].astype(f32)).astype(bf16)
+                    l_copy(i_l, h).start()
 
         @pl.when((i_t >= 0) & (i_t < chunks))
         def _():
             total[i_t] = (
                 part[i_t] + r_in[i_t].astype(f32) + l_in[i_t].astype(f32)).astype(bf16)
 
-    slab_copy(0).wait()
-    half_unit(0, 0)
-    half_unit(0, 1)
+    if by_block:
+        half[0] = acc[...].astype(bf16)
+    else:
+        half_unit(0, 0)
+        half_unit(0, 1)
     part_unit(0)
 
     early = SPLIT - 1
@@ -317,28 +347,47 @@
     across_cores([early])
 
     weighted = (w_sum[...] + weigh(early)) * normalizer
-    e_all[me] = lax.dot_general(
+    e_s[c] = lax.dot_general(
         jnp.broadcast_to(weighted, (8, rows)), onehot[...], (((1,), (1,)), ((), ())),
         precision=lax.Precision.HIGHEST, preferred_element_type=f32)
 
-    def e_copy(slot, peer, dev):
-        return pltpu.make_async_remote_copy(
-            src_ref=e_all.at[slot], dst_ref=e_all.at[slot], send_sem=e_send.at[peer],
-            recv_sem=e_recv.at[slot], device_id=dev, device_id_type=MESH)
-
-    others(lambda idx, dev: e_copy(me, idx, dev).start())
-
+    def es_copy(core):
+        return pltpu.make_async_remote_copy(
+            src_ref=e_s.at[core], dst_ref=e_s.at[core], send_sem=es_send.at[0],
+            recv_sem=es_recv.at[0], device_id={"occ": 1 - c}, device_id_type=MESH)
+
+    def ex_copy(xx, d):
+        return pltpu.make_async_remote_copy(
+            src_ref=e_x.at[xx], dst_ref=e_x.at[xx], send_sem=ex_send.at[d],
+            recv_sem=ex_recv.at[xx], device_id={"aux": lax.rem(x + d, nx)}, device_id_type=MESH)
+
+    def ez_copy(slot, peer):
+        return pltpu.make_async_remote_copy(
+            src_ref=e_z.at[slot], dst_ref=e_z.at[slot], send_sem=ez_send.at[peer],
+            recv_sem=ez_recv.at[slot], device_id={"ao": peer}, device_id_type=MESH)
+
+    es_copy(c).start()
     across_aux([early])
+    es_copy(1 - c).wait_recv()
+    e_x[x] = e_s[0] + e_s[1]
+    for d in range(1, nx):
+        ex_copy(x, d).start()
+    for d in range(1, nx):
+        ex_copy(lax.rem(x + d, nx), d).wait_recv()
+    e_z[z] = sum(e_x[k] for k in range(nx))
+    along_ao(lambda idx, dev: ez_copy(z, idx).start())
     finish([early])
 
     def sent(i, carry):
         @pl.when(z + 1 < n)
         def _():
-            r_copy(i).wait_send()
+            for h in range(PIECES):
+                r_copy(i, h).wait_send()
 
         @pl.when(z > 0)
         def _():
-            l_copy(i).wait_send()
+            for h in range(PIECES):
+                l_copy(i, h).wait_send()
         return carry
 
     lax.fori_loop(0, chunks, sent, 0)
@@ -366,10 +415,12 @@
             s_copy(k, lax.rem(x + d, nx)).wait_send()
         for d in range(1, nx):
             x_copy(k, d).wait_send()
-    others(lambda idx, dev: e_copy(idx, idx, dev).wait_recv())
-    others(lambda idx, dev: e_copy(me, idx, dev).wait_send())
-    energy_out[...] = lax.fori_loop(
-        1, group_size, lambda i, acc: acc + e_all[i], e_all[0])[0]
+    es_copy(c).wait_send()
+    for d in range(1, nx):
+        ex_copy(x, d).wait_send()
+    along_ao(lambda idx, dev: ez_copy(idx, idx).wait_recv())
+    along_ao(lambda idx, dev: ez_copy(z, idx).wait_send())
+    energy_out[...] = lax.fori_loop(1, n, lambda i, value: value + e_z[i], e_z[0])[0]
 
 
 def shards(n, nx, slab, coeffs, atom_of):
@@ -377,7 +428,6 @@
     rows, occ = coeffs.shape
     nu = slab.shape[2]
     chunks, height, width = naux * SPLIT, occ // SPLIT, occ // (nx * 2)
-    group_size = n * nx * 2
     bf16, f32 = jnp.bfloat16, jnp.float32
     third = width // SPLIT
     share = nx if rows % (32 * nx) == 0 else 1
@@ -405,12 +455,15 @@
             pltpu.VMEM((SPLIT, nx, third, rows), bf16),
             pltpu.VMEM((SPLIT, nx, third, rows), bf16),
             pltpu.VMEM((NATOM, rows), f32),
-            pltpu.VMEM((group_size, 8, NATOM), f32),
+            pltpu.VMEM((2, 8, NATOM), f32),
+            pltpu.VMEM((nx, 8, NATOM), f32),
+            pltpu.VMEM((n, 8, NATOM), f32),
             pltpu.VMEM((1, rows), f32),
+            pltpu.VMEM((rows, occ), f32),
             dma(naux), dma(n), dma(n), dma(n),
             dma(n, share), dma(n, share), dma(n, share), dma(n, share),
-            dma(chunks), dma(chunks), dma(chunks), dma(chunks),
-            dma(SPLIT, nx), dma(SPLIT, nx), dma(SPLIT, nx), dma(SPLIT, nx), dma(group_size), dma(group_size),
+            dma(chunks, PIECES), dma(chunks, PIECES), dma(chunks, PIECES), dma(chunks, PIECES),
+            dma(SPLIT, nx), dma(SPLIT, nx), dma(SPLIT, nx), dma(SPLIT, nx), dma(1), dma(1), dma(nx), dma(nx), dma(n), dma(n),
         ],
         compiler_params=pltpu.CompilerParams(
             collective_id=0, has_side_effects=True, vmem_limit_bytes=56 * 1024 * 1024),

time: 84.1 us -> 81.6 us (0.970)
  Pallas kernels: 80.3 us -> 77.8 us
    pallas_call x1, Pallas kernels: 80.3 us -> 77.8 us  [shards(): pl.pallas_call(functools.partial(kernel, (n, nx, naux, share)), out_shape...]
where the time goes in v3:
time: 81.6 us; the launch traced here: 81.4 us
  Pallas kernels  77.8 us (95%)
  local copies, waits for them, and re-layouts  2.95 us (4%)
    pallas_call x1, Pallas kernels, shards(): pl.pallas_call(functools.partial(kernel, (n, nx, naux, share)), out_shape...  77.8 us
    unnamed x2, local copies, waits for them, and re-layouts  2.95 us

profile of v3, /device:TPU:0, one launch (start us, length us, event | category | flops | bytes accessed | tf_op | source)
XLA Modules:
  0.0 81.4 jit_solution(3758403065781000550)
XLA Ops:
  0.6 77.8 %shard_map.50 = (f32[96,768]{1,0:T(8,128)}, f32[400]{0:T(512)}) custom-call(bf16[10,768,3072]{2,1,0:T(8,128)(2,1)} %slab.1, bf16[768,384]{1,0:T(8,128)(2,1)} %coeffs.1, s32[768]{0:T(1024)} %atom_of.1), custom_call_target="tpu_custom_call" | custom-call | flops 11324620800 | bytes 23592960 | tf_op jit(solution)/shard_map/pallas_call | solution.py:438
  78.4 1.7 %copy.7 = f32[768,96]{0,1:T(8,128)} copy(f32[768,96]{0,1:T(8,128)} %bitcast.1) | data formatting | bytes 589824
  80.1 1.3 %copy.8 = f32[400]{0:T(512)} copy(f32[400]{0:T(512)} %get-tuple-element.9) | data formatting | bytes 3200
